TPU v7x, 256 devices: a whole 4x4x8 slice. The times are simulated.
256 devices in a mesh: expert: 32 (over x, z), tensor: 8 (over y, core).
Axes of the slice: x: 4, y: 4, z: 8, core: 2. Of those that a mesh axis runs over, the one named last changes fastest.
Arguments:
- attn_partials: bfloat16 [8, 2, 2048, 4096], P('tensor', None, 'expert'), may hold values from -4 to 4
- resid: bfloat16 [2, 2048, 4096], P(None, 'expert'), may hold values from -6 to 6
- norm_gain: float32 [4096], replicated, may hold values from 0.25 to 1.75
- expert_ids: int32 [2, 2048, 8], P(None, 'expert'), may hold values from 0 to 31, all different within a row; in each aligned block of 8 rows (0 to 7, 8 to 15, ..., all dimensions but the last counted through in order) at most 3 rows name the same one
- gate_num: int32 [2, 2048, 8], P(None, 'expert'), may hold values from 1 to 128
- w_gate: bfloat16 [32, 4096, 3072], P('expert', None, 'tensor'), may hold values from -0.09375 to 0.09375
- w_up: bfloat16 [32, 4096, 3072], P('expert', None, 'tensor'), may hold values from -0.09375 to 0.09375
- w_down: bfloat16 [32, 3072, 4096], P('expert', 'tensor'), may hold values from -0.109375 to 0.109375
Outputs:
- residual_out: bfloat16 [2, 2048, 4096], P(None, ('expert', 'tensor'))
- expert_mix: bfloat16 [2, 2048, 4096], P(None, ('expert', 'tensor'))
Inputs may be any that keep to these rules, and one draw needn't show every extreme that they name: `expert_ids`: each row names 8 different experts. In each aligned block of 8 rows (the rows of one device, branch 0 first), no expert is named by more than 3 rows, a bound that some block reaches.
All inputs are finite; a program needn't handle non-finite values.
Results may differ from a plain program's by a relative error of at most 0.034.
Values may be sent and summed in bfloat16 or wider, within the bound.
A program may use at most 128 MiB of HBM per device.

v0:
```python
import jax
import jax.numpy as jnp
from jax import lax
from jax.sharding import PartitionSpec as P


def route_table(labels, numerators, experts, capacity):
    names = jnp.arange(experts, dtype=jnp.int32)
    hit = labels[..., None] == names
    member = jnp.any(hit, axis=-2).astype(jnp.int32)
    weight = jnp.sum(
        jnp.where(hit, numerators[..., None].astype(jnp.float32) / 128.0, 0.0), axis=-2
    )
    rank = jnp.cumsum(member, axis=-2) - member
    slots = jnp.arange(capacity, dtype=jnp.int32)
    chosen = (member[..., None] == 1) & (rank[..., None] == slots)
    return (chosen, weight)


def rms_scale(hstate, norm_gain):
    meansq = jnp.mean(hstate * hstate, axis=-1, keepdims=True)
    return (hstate * lax.rsqrt(meansq + 1e-06) * norm_gain).astype(jnp.bfloat16)


def shards(attn_partials, resid, norm_gain, expert_ids, gate_num, w_gate, w_up, w_down):
    experts = lax.axis_size("expert")
    tensor_count = lax.axis_size("tensor")
    tensor_index = lax.axis_index("tensor")
    width = resid.shape[2]
    tok_dev = resid.shape[1] // tensor_count
    top = expert_ids.shape[2]
    capacity = min(tok_dev, 3 * tok_dev * top // (2 * experts))
    gate_block = w_gate[0]
    up_block = w_up[0]
    down_block = w_down[0]
    first = tensor_index * tok_dev
    attn_all = lax.psum(attn_partials[0].astype(jnp.float32).astype(jnp.bfloat16), "tensor").astype(
        jnp.float32
    )
    group_state = resid.astype(jnp.float32) + attn_all
    hstate = lax.dynamic_slice_in_dim(group_state, first, tok_dev, 1)
    normed_group = rms_scale(group_state, norm_gain)
    group_labels = expert_ids.reshape(2, tensor_count, tok_dev, top)
    group_nums = gate_num.reshape(2, tensor_count, tok_dev, top)
    chosen_group, weight_group = route_table(group_labels, group_nums, experts, capacity)
    send = jnp.einsum(
        "btiec,btid->tbecd",
        chosen_group.astype(jnp.bfloat16),
        normed_group.reshape(2, tensor_count, tok_dev, width),
        preferred_element_type=jnp.float32,
    ).astype(jnp.bfloat16)
    received = lax.all_to_all(send, "expert", split_axis=2, concat_axis=2, tiled=True)
    piece = received.reshape(-1, width)
    gate = jnp.dot(piece, gate_block, preferred_element_type=jnp.float32)
    up = jnp.dot(piece, up_block, preferred_element_type=jnp.float32)
    hidden = (jax.nn.silu(gate) * up).astype(jnp.bfloat16)
    chosen = lax.dynamic_index_in_dim(chosen_group, tensor_index, 1, keepdims=False)
    weight = lax.dynamic_index_in_dim(weight_group, tensor_index, 1, keepdims=False)
    piece = hidden
    summed = lax.psum_scatter(
        jnp.dot(piece, down_block, preferred_element_type=jnp.float32).astype(jnp.bfloat16),
        "tensor",
        scatter_dimension=0,
        tiled=True,
    )
    outputs = summed.reshape(2, experts, capacity, width)
    back = lax.all_to_all(outputs, "expert", split_axis=1, concat_axis=1, tiled=True)
    weighted = chosen.astype(jnp.float32) * weight[..., None]
    mixed = jnp.einsum(
        "biec,becd->bid", weighted, back.astype(jnp.float32), precision=lax.Precision.HIGHEST
    )
    return (hstate.astype(jnp.bfloat16), mixed.astype(jnp.bfloat16))


def solution(mesh):
    placed = (
        P("tensor", None, "expert", None),
        P(None, "expert", None),
        P(),
        P(None, "expert", None),
        P(None, "expert", None),
        P("expert", None, "tensor"),
        P("expert", None, "tensor"),
        P("expert", "tensor", None),
    )
    return jax.shard_map(
        shards,
        mesh=mesh,
        in_specs=placed,
        out_specs=(P(None, ("expert", "tensor"), None), P(None, ("expert", "tensor"), None)),
        check_vma=False,
    )
```

profile of v0, /device:TPU:1, one launch (start us, length us, event | category | flops | bytes accessed | tf_op | source)
XLA Modules:
  0.0 614.5 jit_solution(9248547080431533688)
XLA Ops:
  7.2 0.7 all-reduce.2.cloned.1.call-update
  8.0 0.9 copy.44
  8.9 0.3 fusion.14
  9.2 0.1 reduce_window_sum.11
  9.3 0.1 fusion.15
  9.3 70.5 %all-reduce.2.cloned.1.call-done = bf16[2,64,4096]{2,1,0:T(8,128)(2,1)} async-done(((bf16[2,64,4096]{2,1,0:T(8,128)(2,1)}), bf16[2,64,4096]{2,1,0:T(8,128)(2,1)}) %all-reduce.2.cloned.1.call-update) | async-done | bytes 1048592 | tf_op jit(solution)/shard_map/psum | solution.py:37
  79.8 2.1 multiply_reduce_fusion
  82.0 3.7 convolution_convert_fusion.1
  85.7 16.0 %copy.38 = bf16[8,2,32,3,4096]{4,0,3,1,2:T(8,128)(2,1)S(1)} copy(bf16[8,2,32,3,4096]{4,2,3,1,0:T(8,128)(2,1)S(1)} %convolution_convert_fusion.1) | data formatting | bytes 25165824 | tf_op jit(solution)/shard_map/convert_element_type | solution.py:51
  101.7 279.8 %all_to_all.10 = bf16[8,2,32,3,4096]{4,0,3,1,2:T(8,128)(2,1)S(1)} all-to-all(bf16[8,2,32,3,4096]{4,0,3,1,2:T(8,128)(2,1)S(1)} %copy.38), channel_id=1, replica_groups=mesh['expert'=32,'tensor'=8] {'expert'}, dimensions={2} | all-to-all | bytes 25165824 | tf_op jit(solution)/shard_map/all_to_all | solution.py:52
  381.6 30.9 %copy.39 = bf16[8,2,32,3,4096]{4,3,2,1,0:T(4,128)(2,1)} copy(bf16[8,2,32,3,4096]{4,0,3,1,2:T(8,128)(2,1)S(1)} %all_to_all.10) | data formatting | bytes 25165824 | tf_op jit(solution)/shard_map/all_to_all | solution.py:52
  412.5 26.2 %reshape.54 = bf16[1536,4096]{1,0:T(8,128)(2,1)} reshape(bf16[8,2,32,3,4096]{4,3,2,1,0:T(4,128)(2,1)} %copy.39) | data formatting | bytes 25165824 | tf_op jit(solution)/shard_map/reshape | solution.py:53
  438.7 11.5 %fusion.3 = f32[1536,384]{1,0:T(8,128)} fusion(bf16[1536,4096]{1,0:T(8,128)(2,1)} %reshape.54, bf16[1,4096,384]{2,1,0:T(8,128)(2,1)} %param.13), kind=kOutput, calls=%fused_computation.7 | convolution fusion | flops 4831838208 | bytes 18087936 | tf_op jit(solution)/shard_map/dot_general | solution.py:54
  450.2 20.1 %convolution_convert_fusion = bf16[1536,4096]{1,0:T(8,128)(2,1)} fusion(bf16[1,384,4096]{2,1,0:T(8,128)(2,1)S(1)} %copy-done, bf16[1536,4096]{1,0:T(8,128)(2,1)} %reshape.54, bf16[1,4096,384]{2,1,0:T(8,128)(2,1)} %param.14, f32[1536,384]{1,0:T(8,128)} %fusion.3), kind=kOutput, calls=%fused_computation | convolution fusion | flops 9673506816 | bytes 33816576 | tf_op jit(solution)/shard_map/dot_general | solution.py:61
  470.3 77.3 %reduce-scatter.2.cloned.1.call-done = bf16[192,4096]{1,0:T(8,128)(2,1)} async-done(((bf16[1536,4096]{1,0:T(8,128)(2,1)}), bf16[192,4096]{1,0:T(8,128)(2,1)}) %reduce-scatter.2.cloned.1.call-update) | async-done | bytes 1572880 | tf_op jit(solution)/shard_map/reduce_scatter | solution.py:60
  547.6 4.1 reshape.55
  551.7 4.8 copy.40
  556.5 10.0 %all-to-all-start.1 = ((bf16[2,32,3,4096]{3,0,2,1:T(2,128)(2,1)}), bf16[2,32,3,4096]{3,0,2,1:T(2,128)(2,1)}, u32[]{:S(2)}, u32[]{:S(2)}) async-start(bf16[2,32,3,4096]{3,0,2,1:T(2,128)(2,1)} %copy.40), calls=%async_computation.2 | async-start | bytes 3145728 | tf_op jit(solution)/shard_map/all_to_all | solution.py:67
  566.5 0.1 copy.45
  566.6 0.4 select_reduce_fusion
  567.0 1.8 convert_add_fusion
  568.8 0.7 dynamic-slice_convert_fusion
  569.4 33.6 %all-to-all-done.1 = bf16[2,32,3,4096]{3,0,2,1:T(2,128)(2,1)} async-done(((bf16[2,32,3,4096]{3,0,2,1:T(2,128)(2,1)}), bf16[2,32,3,4096]{3,0,2,1:T(2,128)(2,1)}, u32[]{:S(2)}, u32[]{:S(2)}) %all-to-all-start.1) | async-done | bytes 1572896 | tf_op jit(solution)/shard_map/all_to_all | solution.py:67
  603.1 4.6 fusion
  (17 shorter events, 0.2 us)
Async XLA Ops:
  7.2 443.1 %copy-start = (bf16[1,384,4096]{2,1,0:T(8,128)(2,1)S(1)}, bf16[1,384,4096]{2,1,0:T(8,128)(2,1)}, u32[]{:S(2)}) copy-start(bf16[1,384,4096]{2,1,0:T(8,128)(2,1)} %param.15) | copy-start | bytes 9437188
  7.2 74.8 %copy-start.3 = (f32[4096]{0:T(1024)S(1)}, f32[4096]{0:T(1024)}, u32[]{:S(2)}) copy-start(f32[4096]{0:T(1024)} %param.10) | copy-start | bytes 49156
  7.2 72.6 %all-reduce.2.cloned.1.call-start = ((), (), s32[]{:S(2)}) async-start(), calls=%async_computation.3 | async-start | bytes 2097152 | tf_op jit(solution)/shard_map/psum | solution.py:37
  7.9 539.7 %reduce-scatter.2.cloned.1.call-start = ((), (), s32[]{:S(2)}) async-start(), calls=%async_computation.4 | async-start | bytes 14155776 | tf_op jit(solution)/shard_map/reduce_scatter | solution.py:60
  79.8 2.1 copy-start.1
  79.8 2.2 copy-start.2
  556.5 10.0 %copy-start.4 = (s32[2,64,8]{1,2,0:T(8,128)S(1)}, s32[2,64,8]{1,2,0:T(8,128)}, u32[]{:S(2)}) copy-start(s32[2,64,8]{1,2,0:T(8,128)} %param.12) | copy-start | bytes 12292
  556.5 46.6 %all-to-all-start.1 = ((bf16[2,32,3,4096]{3,0,2,1:T(2,128)(2,1)}), bf16[2,32,3,4096]{3,0,2,1:T(2,128)(2,1)}, u32[]{:S(2)}, u32[]{:S(2)}) async-start(bf16[2,32,3,4096]{3,0,2,1:T(2,128)(2,1)} %copy.40), calls=%async_computation.2 | async-start | bytes 3145728 | tf_op jit(solution)/shard_map/all_to_all | solution.py:67
Sparse Core Ops, SparseCore 0:
  10.4 69.3 all-reduce.1
  470.5 77.1 reduce-scatter.1
where the time goes:
time: 617 us; the launch traced here: 614 us
  blocking collectives  280 us (45%)
  waiting for transfers between devices  182 us (29%)
  local copies, waits for them, and re-layouts  83.8 us (14%)
  matrix products  39.9 us (6%)
  between operations  14.2 us (2%)
  starting transfers between devices  10.1 us (2%)
    all_to_all x1, blocking collectives, shards(): lax.all_to_all(send, 'expert', split_axis=2, concat_axis=2, tiled=True)  280 us
    reduce_scatter x1, waiting for transfers between devices, shards(): lax.psum_scatter(jnp.dot(piece, down_block, preferred_element_type=jnp.fl...  77.3 us
    psum x1, waiting for transfers between devices, shards(): lax.psum(attn_partials[0].astype(jnp.float32).astype(jnp.bfloat16), 'tens...  70.5 us
    all_to_all x1, waiting for transfers between devices, shards(): lax.all_to_all(outputs, 'expert', split_axis=1, concat_axis=1, tiled=True)  33.6 us
    all_to_all x1, local copies, waits for them, and re-layouts, shards(): lax.all_to_all(send, 'expert', split_axis=2, concat_axis=2, tiled=True)  30.9 us
    reshape x1, local copies, waits for them, and re-layouts, shards(): piece = received.reshape(-1, width)  26.2 us
    dot_general x1, matrix products, shards(): jnp.dot(piece, down_block, preferred_element_type=jnp.float32)  20.1 us
    convert_element_type x1, local copies, waits for them, and re-layouts, shards(): send = jnp.einsum('btiec,btid->tbecd', chosen_group.astype(jnp.bfloat16),...  16 us
  transfers between devices with their start and end apart: 3, of which 3 were waited for; matrix products, arithmetic and copies ran while one was open for 1% of the time, Pallas kernels for 0%

commit v1 on v0

v1 whole, which is shorter than its diff:
```python
import functools

import jax
import jax.numpy as jnp
from jax import lax
from jax.experimental import pallas as pl
from jax.experimental.pallas import tpu as pltpu
from jax.sharding import PartitionSpec as P

MESH = pl.DeviceIdType.MESH
BF16 = jnp.bfloat16
F32 = jnp.float32
BLOCK = 8


def grid_of(experts):
    return (4, experts // 4) if experts >= 4 else (1, experts)


def groups_of(nz):
    if nz == 8:
        return ((0, 1), (4, -2), (3, -3), (2, -1))
    return tuple((dz,) for dz in range(nz))


def kernel(
    cfg,
    attn, resid, gain, ids, nums, wg, wu, wd,
    out_res, out_mix,
    wgu, wdv, ap, arb, atr, afin, rsd, hs, nrm, rsend, rbuf, ssend, sbuf,
    rank, gate, sel, selw, snd, xg, acc, hid, own, sib, rb, tr, fin, back, msend, mbuf,
    lsem, ssem, rsem,
):
    experts, nt, nx, nz, cap, d = cfg
    ny = nt // 2
    dc = d // nt
    tg = attn.shape[0]
    per = tg // nt
    f = wg.shape[1]
    nb = tg // BLOCK
    sl = nb * cap

    e = lax.axis_index("expert")
    t = lax.axis_index("tensor")
    x, z = e // nz, lax.rem(e, nz)
    y, c = t // 2, lax.rem(t, 2)
    step = 1 - 2 * c
    yf = lax.rem(y + step + ny, ny)
    yb = lax.rem(y - step + ny, ny)
    yo = lax.rem(y + 2, ny)
    sibling = (e, y * 2 + 1 - c)
    ahead = (e, yf * 2 + c)
    behind = (e, yb * 2 + c)

    offsets, groups = [], []
    for dzs in groups_of(nz):
        start = len(offsets)
        for dz in dzs:
            for dx in range(nx):
                offsets.append((dx, dz % nz))
        groups.append((start, len(offsets)))

    def expert_at(k, sign=1):
        dx, dz = offsets[k]
        ex = lax.rem(x + (dx if sign > 0 else nx - dx), nx)
        ez = lax.rem(z + (dz if sign > 0 else nz - dz), nz)
        return ex * nz + ez

    counter = {"l": 0, "s": 0, "r": 0}
    sent = []

    def fresh(kind):
        counter[kind] += 1
        return counter[kind] - 1

    def local(src, dst):
        return pltpu.make_async_copy(src, dst, lsem.at[fresh("l")])

    def remote(src, dst, device):
        copy = pltpu.make_async_remote_copy(
            src_ref=src, dst_ref=dst, send_sem=ssem.at[fresh("s")], recv_sem=rsem.at[fresh("r")],
            device_id=device, device_id_type=MESH,
        )
        copy.start()
        sent.append(copy)
        return copy

    barrier = pltpu.get_barrier_semaphore()
    peers = 0
    for k, (dx, dz) in enumerate(offsets):
        if (dx, dz) != (0, 0):
            pl.semaphore_signal(barrier, inc=1, device_id=(expert_at(k), t), device_id_type=MESH)
            peers += 1
    for i in range(1, nt):
        pl.semaphore_signal(barrier, inc=1, device_id=(e, lax.rem(t + i, nt)), device_id_type=MESH)
        peers += 1

    def cols(ref, j):
        return ref.at[:, pl.ds(pl.multiple_of(j * dc, dc), dc)]

    own_loads = [local(cols(attn, 2 * yy + c), ap.at[yy]) for yy in range(ny)]
    own_loads.append(local(cols(resid, t), rsd))
    for copy in own_loads:
        copy.start()
    w_loads = [local(wg, wgu.at[:, pl.ds(0, f)]), local(wu, wgu.at[:, pl.ds(f, f)])]
    for j in range(nt):
        w_loads.append(local(wd.at[:, pl.ds(j * dc, dc)], wdv.at[j]))
    for copy in w_loads:
        copy.start()

    pl.semaphore_wait(barrier, peers)

    a1 = [remote(cols(attn, 2 * yy + 1 - c), arb.at[yy], sibling) for yy in range(ny)]

    lane = lax.broadcasted_iota(jnp.int32, (experts, tg), 0)
    member = jnp.zeros((experts, tg), F32)
    weight = jnp.zeros((experts, tg), F32)
    for k in range(ids.shape[0]):
        hit = ids[k : k + 1, :] == lane
        member = member + jnp.where(hit, 1.0, 0.0)
        weight = weight + jnp.where(hit, nums[k : k + 1, :].astype(F32) / 128.0, 0.0)
    ri = lax.broadcasted_iota(jnp.int32, (tg, tg), 0)
    ci = lax.broadcasted_iota(jnp.int32, (tg, tg), 1)
    lower = jnp.where((ri // BLOCK == ci // BLOCK) & (ri < ci), 1.0, 0.0).astype(BF16)
    before = jnp.dot(member.astype(BF16), lower, preferred_element_type=F32)
    rank[...] = jnp.where(member > 0.5, before, -1.0)
    gate[...] = weight
    ji = lax.broadcasted_iota(jnp.int32, (sl, tg), 0)
    bi = lax.broadcasted_iota(jnp.int32, (sl, tg), 1) // BLOCK
    jd = jnp.zeros((sl, tg), jnp.int32)
    for m in range(1, nb):
        jd = jd + jnp.where(ji >= m * cap, 1, 0)
    want = jnp.where(jd == bi, (ji - jd * cap).astype(F32), -2.0)
    for k in range(experts):
        at = pl.ds(expert_at(k), 1)
        chosen = want == rank[at, :]
        sel[k * sl : (k + 1) * sl, :] = jnp.where(chosen, 1.0, 0.0).astype(BF16)
        selw[k * sl : (k + 1) * sl, :] = jnp.where(chosen, gate[at, :], 0.0).astype(BF16)

    for copy in own_loads:
        copy.wait()
    for copy in a1:
        copy.wait_recv()

    def add_to(ref, i, *others):
        total = ref[i].astype(F32)
        for other in others:
            total = total + other.astype(F32)
        ref[i] = total.astype(BF16)

    add_to(ap, yo, arb[yo])
    a2 = remote(ap.at[yo], atr, ahead)
    add_to(ap, yb, arb[yb])
    a3 = remote(ap.at[yb], afin.at[1], behind)
    add_to(ap, yf, arb[yf])
    a2.wait_recv()
    add_to(ap, yf, atr[...])
    a4 = remote(ap.at[yf], afin.at[0], ahead)
    mine = ap[y].astype(F32) + arb[y].astype(F32) + rsd[...].astype(F32)
    a3.wait_recv()
    mine = mine + afin[1].astype(F32)
    a4.wait_recv()
    mine = mine + afin[0].astype(F32)
    half = tg // 2
    state = jnp.concatenate(
        [
            mine[b * half + i * BLOCK : b * half + (i + 1) * BLOCK]
            for i in range(nt)
            for b in range(2)
        ],
        axis=0,
    )
    hs[...] = state

    part = jnp.sum(state * state, axis=1, keepdims=True)
    ssend[...] = jnp.transpose(jnp.broadcast_to(part, (tg, tg)))[:8]
    sums = []
    for i in range(1, nt):
        sums.append(remote(ssend, sbuf.at[t], (e, lax.rem(t + i, nt))))
    sbuf[t] = ssend[...]
    rsend[...] = state.astype(BF16)

    def to_rows(src, dst):
        copies = []
        for i in range(1, nt):
            to = lax.rem(t + i, nt)
            rows = pl.ds(pl.multiple_of(to * per, per), per)
            copies.append(remote(src.at[rows], dst.at[t], (e, to)))
        keep = local(src.at[pl.ds(pl.multiple_of(t * per, per), per)], dst.at[t])
        keep.start()
        return copies, keep

    for copy in sums:
        copy.wait_recv()
    total = sbuf[0]
    for i in range(1, nt):
        total = total + sbuf[i]
    total = jnp.transpose(jnp.concatenate([total] * (tg // 8), axis=0))
    scale = lax.rsqrt(total * (1.0 / d) + 1e-06)
    mygain = gain[pl.ds(t, 1), :]
    for j in range(dc // tg):
        at = slice(j * tg, (j + 1) * tg)
        nrm[:, at] = (hs[:, at] * scale * mygain[:, at]).astype(BF16)

    there = [None] * experts
    for k0, k1 in groups:
        rows = slice(k0 * sl, k1 * sl)
        snd[rows, :] = jnp.dot(sel[rows, :], nrm[...], preferred_element_type=F32).astype(BF16)
        for k in range(k0, k1):
            at = pl.ds(k * sl, sl)
            if offsets[k] == (0, 0):
                there[k] = local(snd.at[at], xg.at[t, at])
                there[k].start()
            else:
                there[k] = remote(snd.at[at], xg.at[t, at], (expert_at(k), t))
    res_rows = to_rows(rsend, rbuf)

    def arrived(k, copies):
        if offsets[k] == (0, 0):
            copies[k].wait()
        else:
            copies[k].wait_recv()

    state_of = [dict() for _ in groups]

    def span(g):
        k0, k1 = groups[g]
        return k0 * sl, (k1 - k0) * sl

    def gather_first(g):
        s = state_of[g]
        r0, rn = span(g)
        for k in range(*groups[g]):
            arrived(k, there)
        block = xg.at[t, pl.ds(r0, rn)]
        s["b"] = remote(block, block, ahead)
        s["f"] = remote(block, block, behind)
        s["near"] = [remote(block, block, sibling)]

    def gather_second(g):
        s = state_of[g]
        r0, rn = span(g)
        s["b"].wait_recv()
        block = xg.at[yb * 2 + c, pl.ds(r0, rn)]
        s["o"] = remote(block, block, ahead)
        s["near"].append(remote(block, block, sibling))
        s["f"].wait_recv()
        block = xg.at[yf * 2 + c, pl.ds(r0, rn)]
        s["near"].append(remote(block, block, sibling))

    def gather_third(g):
        s = state_of[g]
        r0, rn = span(g)
        s["o"].wait_recv()
        block = xg.at[yo * 2 + c, pl.ds(r0, rn)]
        s["near"].append(remote(block, block, sibling))

    def compute(g):
        s = state_of[g]
        r0, rn = span(g)
        for copy in s["near"]:
            copy.wait_recv()
        if g == 0:
            for copy in w_loads:
                copy.wait()
        at = pl.ds(r0, rn)
        acc[:rn, :] = jnp.zeros((rn, 2 * f), F32)

        @pl.loop(0, nt)
        def _(j):
            w = wgu[pl.ds(pl.multiple_of(j * dc, dc), dc), :]
            acc[:rn, :] += jnp.dot(xg[j, at, :], w, preferred_element_type=F32)

        a = acc[:rn, :f]
        hid[:rn, :] = (a / (1.0 + jnp.exp(-a)) * acc[:rn, f:]).astype(BF16)

        @pl.loop(0, ny)
        def _(yy):
            sib[yy, at, :] = jnp.dot(
                hid[:rn, :], wdv[yy * 2 + 1 - c], preferred_element_type=F32
            ).astype(BF16)

        s["pair"] = remote(sib.at[:, at], rb.at[:, at], sibling)

        @pl.loop(0, ny)
        def _(yy):
            own[yy, at, :] = jnp.dot(
                hid[:rn, :], wdv[yy * 2 + c], preferred_element_type=F32
            ).astype(BF16)

    def reduce_first(g):
        s = state_of[g]
        r0, rn = span(g)
        at = pl.ds(r0, rn)
        s["pair"].wait_recv()

        def pair(i):
            own[i, at, :] = (own[i, at, :].astype(F32) + rb[i, at, :].astype(F32)).astype(BF16)

        pair(yo)
        s["t"] = remote(own.at[yo, at], tr.at[at], ahead)
        pair(yb)
        s["f1"] = remote(own.at[yb, at], fin.at[1, at], behind)
        pair(yf)
        pair(y)

    def reduce_second(g):
        s = state_of[g]
        r0, rn = span(g)
        at = pl.ds(r0, rn)
        s["t"].wait_recv()
        own[yf, at, :] = (own[yf, at, :].astype(F32) + tr[at, :].astype(F32)).astype(BF16)
        s["f0"] = remote(own.at[yf, at], fin.at[0, at], ahead)

    back_copies = [None] * experts

    def reduce_third(g):
        s = state_of[g]
        r0, rn = span(g)
        at = pl.ds(r0, rn)
        s["f1"].wait_recv()
        s["f0"].wait_recv()
        own[y, at, :] = (
            own[y, at, :].astype(F32) + fin[0, at, :].astype(F32) + fin[1, at, :].astype(F32)
        ).astype(BF16)
        for k in range(*groups[g]):
            here = pl.ds(k * sl, sl)
            if offsets[k] == (0, 0):
                back_copies[k] = local(own.at[y, here], back.at[here])
                back_copies[k].start()
            else:
                back_copies[k] = remote(own.at[y, here], back.at[here], (expert_at(k, -1), t))

    n = len(groups)
    gather_first(0)
    gather_second(0)
    if n > 1:
        gather_first(1)
    gather_third(0)
    compute(0)
    for g in range(1, n):
        gather_second(g)
        reduce_first(g - 1)
        gather_third(g)
        if g + 1 < n:
            gather_first(g + 1)
        reduce_second(g - 1)
        if g >= 2:
            reduce_third(g - 2)
        compute(g)
    reduce_first(n - 1)
    if n > 1:
        reduce_third(n - 2)
    reduce_second(n - 1)
    reduce_third(n - 1)

    def to_out(copies, buf, out):
        for copy in copies[0]:
            copy.wait_recv()
        copies[1].wait()
        for j in range(nt):
            out[:, j * dc : (j + 1) * dc] = buf[j]

    to_out(res_rows, rbuf, out_res)

    mixed = jnp.zeros((tg, dc), F32)
    for k0, k1 in groups:
        for k in range(k0, k1):
            arrived(k, back_copies)
        rows = slice(k0 * sl, k1 * sl)
        mixed = mixed + lax.dot_general(
            selw[rows, :], back[rows, :], (((0,), (0,)), ((), ())), preferred_element_type=F32
        )
    msend[...] = mixed.astype(BF16)
    to_out(to_rows(msend, mbuf), mbuf, out_mix)
    for copy in sent:
        copy.wait_send()


def shards(attn_partials, resid, norm_gain, expert_ids, gate_num, w_gate, w_up, w_down):
    experts = lax.axis_size("expert")
    nt = lax.axis_size("tensor")
    nx, nz = grid_of(experts)
    _, two, tokens, d = attn_partials.shape
    top = expert_ids.shape[-1]
    tg = two * tokens
    per = tg // nt
    dc = d // nt
    ny = nt // 2
    f = w_gate.shape[-1]
    cap = min(BLOCK, 3 * BLOCK * top // (2 * experts))
    sl = tg // BLOCK * cap
    rows = experts * sl
    most = max(len(g) for g in groups_of(nz)) * nx * sl
    n_groups = len(groups_of(nz))

    def by_device(a):
        a = a.reshape(two, nt, tokens // nt, top)
        return a.transpose(3, 1, 0, 2).reshape(top, tg)

    n_remote = 4 + 3 + 2 * (experts - 1) + 3 * (nt - 1) + 12 * n_groups + ny
    n_local = ny + 3 + nt + 4
    vmem = pl.BlockSpec(memory_space=pltpu.VMEM)
    hbm = pl.BlockSpec(memory_space=pl.ANY)
    scratch = [
        pltpu.VMEM((d, 2 * f), BF16),
        pltpu.VMEM((nt, f, dc), BF16),
        pltpu.VMEM((ny, tg, dc), BF16),
        pltpu.VMEM((ny, tg, dc), BF16),
        pltpu.VMEM((tg, dc), BF16),
        pltpu.VMEM((2, tg, dc), BF16),
        pltpu.VMEM((tg, dc), BF16),
        pltpu.VMEM((tg, dc), F32),
        pltpu.VMEM((tg, dc), BF16),
        pltpu.VMEM((tg, dc), BF16),
        pltpu.VMEM((nt, per, dc), BF16),
        pltpu.VMEM((8, tg), F32),
        pltpu.VMEM((nt, 8, tg), F32),
        pltpu.VMEM((experts, tg), F32),
        pltpu.VMEM((experts, tg), F32),
        pltpu.VMEM((rows, tg), BF16),
        pltpu.VMEM((rows, tg), BF16),
        pltpu.VMEM((rows, dc), BF16),
        pltpu.VMEM((nt, rows, dc), BF16),
        pltpu.VMEM((most, 2 * f), F32),
        pltpu.VMEM((most, f), BF16),
        pltpu.VMEM((ny, rows, dc), BF16),
        pltpu.VMEM((ny, rows, dc), BF16),
        pltpu.VMEM((ny, rows, dc), BF16),
        pltpu.VMEM((rows, dc), BF16),
        pltpu.VMEM((2, rows, dc), BF16),
        pltpu.VMEM((rows, dc), BF16),
        pltpu.VMEM((tg, dc), BF16),
        pltpu.VMEM((nt, per, dc), BF16),
        pltpu.SemaphoreType.DMA((n_local,)),
        pltpu.SemaphoreType.DMA((n_remote,)),
        pltpu.SemaphoreType.DMA((n_remote,)),
    ]
    res, mix = pl.pallas_call(
        functools.partial(kernel, (experts, nt, nx, nz, cap, d)),
        out_shape=[jax.ShapeDtypeStruct((per, d), BF16)] * 2,
        in_specs=[hbm, hbm, vmem, vmem, vmem, hbm, hbm, hbm],
        out_specs=[vmem, vmem],
        scratch_shapes=scratch,
        compiler_params=pltpu.CompilerParams(
            collective_id=0, has_side_effects=True, vmem_limit_bytes=60 * 1024 * 1024
        ),
        cost_estimate=pl.CostEstimate(
            flops=6 * rows * d * f, bytes_accessed=6 * d * f, transcendentals=rows * f
        ),
    )(
        attn_partials.reshape(tg, d),
        resid.reshape(tg, d),
        norm_gain.reshape(nt, dc),
        by_device(expert_ids),
        by_device(gate_num),
        w_gate.reshape(d, f),
        w_up.reshape(d, f),
        w_down.reshape(f, d),
    )
    return (res.reshape(two, per // two, d), mix.reshape(two, per // two, d))


def solution(mesh):
    placed = (
        P("tensor", None, "expert", None),
        P(None, "expert", None),
        P(),
        P(None, "expert", None),
        P(None, "expert", None),
        P("expert", None, "tensor"),
        P("expert", None, "tensor"),
        P("expert", "tensor", None),
    )
    return jax.shard_map(
        shards,
        mesh=mesh,
        in_specs=placed,
        out_specs=(P(None, ("expert", "tensor"), None), P(None, ("expert", "tensor"), None)),
        check_vma=False,
    )
```

time: 617 us -> 187 us (0.30)
  blocking collectives: 280 us -> 0 us
  waiting for transfers between devices: 182 us -> 0 us
  Pallas kernels: 0 us -> 179 us
  local copies, waits for them, and re-layouts: 83.8 us -> 7.57 us
  matrix products: 39.9 us -> 0 us
  between operations: 14.2 us -> 0.67 us
  starting transfers between devices: 10.1 us -> 0 us
    all_to_all x1 -> x0, blocking collectives: 280 us -> none  [shards(): lax.all_to_all(send, 'expert', split_axis=2, concat_axis=2, tiled=True)]
    pallas_call x0 -> x1, Pallas kernels: none -> 179 us  [shards(): pl.pallas_call(functools.partial(kernel, (experts, nt, nx, nz, cap, d)),...]
    reduce_scatter x1 -> x0, waiting for transfers between devices: 77.3 us -> none  [shards(): lax.psum_scatter(jnp.dot(piece, down_block, preferred_element_type=jnp.fl...]
    psum x1 -> x0, waiting for transfers between devices: 70.5 us -> none  [shards(): lax.psum(attn_partials[0].astype(jnp.float32).astype(jnp.bfloat16), 'tens...]
    dot_general x4 -> x0, matrix products: 39.9 us -> none  [the longest x1 20.1 us: shards(): jnp.dot(piece, down_block, preferred_element_type=jnp.float32)]
    all_to_all x1 -> x0, waiting for transfers between devices: 33.6 us -> none  [shards(): lax.all_to_all(outputs, 'expert', split_axis=1, concat_axis=1, tiled=True)]
    all_to_all x1 -> x0, local copies, waits for them, and re-layouts: 30.9 us -> none  [shards(): lax.all_to_all(send, 'expert', split_axis=2, concat_axis=2, tiled=True)]
    reshape x3 -> x7, local copies, waits for them, and re-layouts: 35 us -> 4.43 us  [the longest x4 1.65 us: by_device(): a = a.reshape(two, nt, tokens // nt, top)]
  transfers between devices with their start and end apart: 3 -> 0, of which waited for: 3 -> 0; matrix products, arithmetic and copies ran while one was open for 1% -> 0% of each run, Pallas kernels for 0% -> 0%
where the time goes in v1:
time: 187 us
  Pallas kernels  179 us (96%)
  local copies, waits for them, and re-layouts  7.57 us (4%)
    pallas_call x1, Pallas kernels, shards(): pl.pallas_call(functools.partial(kernel, (experts, nt, nx, nz, cap, d)),...  179 us

profile of v1, /device:TPU:1, one launch (start us, length us, event | category | flops | bytes accessed | tf_op | source)
XLA Modules:
  0.0 187.0 jit_solution(17353532368098841817)
XLA Ops:
  0.6 1.3 reshape.42.gain
  2.0 0.8 reshape.43
  2.7 0.1 copy.15
  2.8 0.7 reshape.44.ids
  3.5 0.8 reshape.45
  4.3 0.1 copy.14
  4.4 0.7 reshape.46.nums
  5.1 178.8 %shard_map.95 = (bf16[16,4096]{1,0:T(8,128)(2,1)}, bf16[16,4096]{1,0:T(8,128)(2,1)}) custom-call(bf16[128,4096]{1,0:T(8,128)(2,1)} %bitcast.24, bf16[128,4096]{1,0:T(8,128)(2,1)} %bitcast.25, f32[8,512]{1,0:T(8,128)} %reshape.42.gain, s32[8,128]{1,0:T(8,128)} %reshape.44.ids, s32[8,128]{1,0:T(8,128)} %reshape.46.nums, bf16[4096,384]{1,0:T(8,128)(2,1)} %bitcast.21, ...), custom_call_target="tpu_custom_call" | custom-call | flops 14495514624 | bytes 9437184 | tf_op jit(solution)/shard_map/pallas_call | solution.py:439
  183.9 1.6 copy.18
  185.5 1.6 copy.19

commit v2 on v1

v2 whole, which is shorter than its diff:
```python
import functools
import re

import jax
import jax.numpy as jnp
from jax import lax
from jax.experimental import pallas as pl
from jax.experimental.pallas import tpu as pltpu
from jax.sharding import PartitionSpec as P

MESH = pl.DeviceIdType.MESH
BF16 = jnp.bfloat16
F32 = jnp.float32
BLOCK = 8


NORMAL = "A3B2A2A4B3A1"
DIRECT = "A0B1"
SCHEDULE = (
    "P5A0P1P4P3D5P2P6D1F5P7D4H5F1P0F4D6D3C5D2H4C6F3Q5",
    "C4D7H1F2Q6H3Q4C7D0H2C3T4Q7F0Q3C2H0T5U4T3Q2C0U5U3",
    "Q0T2C1T0Q1U2U0T1V0U1W3W0W5W4W2W1",
)


def grid_of(experts):
    return (4, experts // 4) if experts >= 4 else (1, experts)


def groups_of(nx, nz):
    def offsets(name):
        far = int(name[1])
        if far in (0, nz - far):
            return [(dx, far) for dx in range(nx)]
        flip = name[0] == "B"
        return [(dx, far if (dx < nx // 2) != flip else nz - far) for dx in range(nx)]

    if nx == 4 and nz == 8:
        return [offsets(a + b) for a, b in zip(NORMAL[::2], NORMAL[1::2])], [
            offsets(a + b) for a, b in zip(DIRECT[::2], DIRECT[1::2])
        ]
    return [[(dx, dz) for dx in range(nx)] for dz in range(1, nz)], [offsets("A0")]


def schedule_of(normal, direct):
    if normal == len(NORMAL) // 2 and direct == len(DIRECT) // 2:
        return [(name, int(g)) for name, g in re.findall("([A-Z])([0-9])", "".join(SCHEDULE))]
    steps = [("A", 0)] + [("P", g) for g in range(normal + direct)]
    for names, groups in (("DFHCQTUW", range(normal)), ("DCQ", range(normal, normal + direct))):
        steps += [(name, g) for name in names for g in groups]
    return steps + [("V", 0)]


def kernel(
    cfg,
    attn, resid, gain, ids, nums, wg, wu, wd,
    outs,
    wgu, wdv, ap, arb, afin, rsd, hs, nall, rsend, rbuf, ssend, sbuf,
    rank, gate, sel, selw, snd, snd4, xg, acc, hid, own, sib, rb, tr, fin, back, back4, msd, mrd, mine4, mix, msend, mbuf,
    lsem, ssem, rsem,
):
    experts, nt, nx, nz, cap, d = cfg
    ny = nt // 2
    dc = d // nt
    tg = attn.shape[0]
    per = tg // nt
    f = wg.shape[1]
    nb = tg // BLOCK
    sl = nb * cap

    e = lax.axis_index("expert")
    t = lax.axis_index("tensor")
    x, z = e // nz, lax.rem(e, nz)
    y, c = t // 2, lax.rem(t, 2)
    step = 1 - 2 * c
    yf = lax.rem(y + step + ny, ny)
    yb = lax.rem(y - step + ny, ny)
    yo = lax.rem(y + 2, ny)
    sibling = (e, y * 2 + 1 - c)
    ahead = (e, yf * 2 + c)
    behind = (e, yb * 2 + c)
    opposite = (e, yo * 2 + c)

    offsets, groups = [], []
    normal, direct = groups_of(nx, nz)
    n = len(normal)
    for members in normal + direct:
        groups.append((len(offsets), len(offsets) + len(members)))
        offsets.extend(members)
    kd = groups[n][0]
    rd0 = kd * sl

    def expert_at(k, sign=1):
        dx, dz = offsets[k]
        ex = lax.rem(x + (dx if sign > 0 else nx - dx), nx)
        ez = lax.rem(z + (dz if sign > 0 else nz - dz), nz)
        return ex * nz + ez

    counter = {"l": 0, "s": 0, "r": 0}
    sent = []

    def fresh(kind):
        counter[kind] += 1
        return counter[kind] - 1

    def local(src, dst):
        return pltpu.make_async_copy(src, dst, lsem.at[fresh("l")])

    def remote(src, dst, device):
        copy = pltpu.make_async_remote_copy(
            src_ref=src, dst_ref=dst, send_sem=ssem.at[fresh("s")], recv_sem=rsem.at[fresh("r")],
            device_id=device, device_id_type=MESH,
        )
        copy.start()
        sent.append(copy)
        return copy

    barrier = pltpu.get_barrier_semaphore()
    peers = 0
    for k, (dx, dz) in enumerate(offsets):
        if (dx, dz) != (0, 0):
            pl.semaphore_signal(barrier, inc=1, device_id=(expert_at(k), t), device_id_type=MESH)
            peers += 1
    for i in range(1, nt):
        pl.semaphore_signal(barrier, inc=1, device_id=(e, lax.rem(t + i, nt)), device_id_type=MESH)
        peers += 1

    def cols(ref, j):
        return ref.at[:, pl.ds(pl.multiple_of(j * dc, dc), dc)]

    own_loads = [local(cols(attn, 2 * yy + c), ap.at[yy]) for yy in (yo, yb, yf, y)]
    own_loads.append(local(cols(resid, t), rsd))
    for copy in own_loads:
        copy.start()
    w_loads = [local(wg, wgu.at[:, pl.ds(0, f)]), local(wu, wgu.at[:, pl.ds(f, f)])]
    for j in range(nt):
        w_loads.append(local(wd.at[:, pl.ds(j * dc, dc)], wdv.at[j]))
    for copy in w_loads:
        copy.start()

    pl.semaphore_wait(barrier, peers)

    a1 = [remote(cols(attn, 2 * yy + 1 - c), arb.at[yy], sibling) for yy in (yo, yf, yb, y)]

    half = tg // 2
    ri = lax.broadcasted_iota(jnp.int32, (tg, tg), 0)
    ci = lax.broadcasted_iota(jnp.int32, (tg, tg), 1)
    branch = lax.rem(ci // BLOCK, 2)
    place = branch * half + ci // (2 * BLOCK) * BLOCK + lax.rem(ci, BLOCK)
    order = jnp.where(ri == place, 1.0, 0.0).astype(BF16)

    def by_device(ref):
        return sum(
            jnp.dot(
                ref[b].astype(F32).astype(BF16),
                order[b * half : (b + 1) * half],
                preferred_element_type=F32,
            )
            for b in range(2)
        )

    names, amounts = by_device(ids), by_device(nums)
    lane = lax.broadcasted_iota(jnp.int32, (experts, tg), 0).astype(F32)
    member = jnp.zeros((experts, tg), F32)
    weight = jnp.zeros((experts, tg), F32)
    for k in range(ids.shape[1]):
        hit = names[k : k + 1, :] == lane
        member = member + jnp.where(hit, 1.0, 0.0)
        weight = weight + jnp.where(hit, amounts[k : k + 1, :] * (1.0 / 128.0), 0.0)
    lower = jnp.where((ri // BLOCK == ci // BLOCK) & (ri < ci), 1.0, 0.0).astype(BF16)
    before = jnp.dot(member.astype(BF16), lower, preferred_element_type=F32)
    rank[...] = jnp.where(member > 0.5, before, -1.0)
    gate[...] = weight
    ji = lax.broadcasted_iota(jnp.int32, (sl, tg), 0)
    bi = lax.broadcasted_iota(jnp.int32, (sl, tg), 1) // BLOCK
    jd = jnp.zeros((sl, tg), jnp.int32)
    for m in range(1, nb):
        jd = jd + jnp.where(ji >= m * cap, 1, 0)
    want = jnp.where(jd == bi, (ji - jd * cap).astype(F32), -2.0)
    for k in range(experts):
        at = pl.ds(expert_at(k), 1)
        chosen = want == rank[at, :]
        sel[k * sl : (k + 1) * sl, :] = jnp.where(chosen, 1.0, 0.0).astype(BF16)
        selw[k * sl : (k + 1) * sl, :] = jnp.where(chosen, gate[at, :], 0.0).astype(BF16)

    a2 = []
    for i, (yy, peer) in enumerate(((yo, opposite), (yb, behind), (yf, ahead))):
        own_loads[i].wait()
        a1[i].wait_recv()
        ap[yy] = ap[yy] + arb[yy]
        a2.append(remote(ap.at[yy], afin.at[i], peer))
    for copy in own_loads[3:]:
        copy.wait()
    a1[3].wait_recv()
    mine = ap[y].astype(F32) + arb[y].astype(F32) + rsd[...].astype(F32)
    for i, copy in enumerate(a2):
        copy.wait_recv()
        mine = mine + afin[i].astype(F32)
    state = jnp.concatenate(
        [
            mine[b * half + i * BLOCK : b * half + (i + 1) * BLOCK]
            for i in range(nt)
            for b in range(2)
        ],
        axis=0,
    )
    hs[...] = state

    part = jnp.sum(state * state, axis=1, keepdims=True)
    ssend[...] = jnp.transpose(jnp.broadcast_to(part, (tg, tg)))[:8]
    sums = []
    for i in range(1, nt):
        sums.append(remote(ssend, sbuf.at[t], (e, lax.rem(t + i, nt))))
    sbuf[t] = ssend[...]
    rsend[...] = state.astype(BF16)

    def to_rows(src, dst):
        copies = []
        for i in range(1, nt):
            to = lax.rem(t + i, nt)
            rows = pl.ds(pl.multiple_of(to * per, per), per)
            copies.append(remote(src.at[rows], dst.at[t], (e, to)))
        keep = local(src.at[pl.ds(pl.multiple_of(t * per, per), per)], dst.at[t])
        keep.start()
        return copies, keep

    res_rows = to_rows(rsend, rbuf)
    for copy in sums:
        copy.wait_recv()
    total = sbuf[0]
    for i in range(1, nt):
        total = total + sbuf[i]
    total = jnp.transpose(jnp.concatenate([total] * (tg // 8), axis=0))
    scale = lax.rsqrt(total * (1.0 / d) + 1e-06)
    mygain = gain[:, pl.ds(pl.multiple_of(t * dc, dc), dc)]
    for j in range(dc // tg):
        at = slice(j * tg, (j + 1) * tg)
        nall[y, :, at] = (hs[:, at] * scale * mygain[:, at]).astype(BF16)

    there = [None] * experts

    spread = []

    def spread_rows(g):
        for peer in (opposite, behind, ahead):
            spread.append(remote(nall.at[y], nall.at[y], peer))

    def move(k, src, dst, device):
        if offsets[k] == (0, 0):
            copy = local(src, dst)
            copy.start()
            return copy
        return remote(src, dst, device)

    def dispatch(g):
        k0, k1 = groups[g]
        rows = slice(k0 * sl, k1 * sl)
        if g < n:
            snd[rows, :] = jnp.dot(sel[rows, :], nall[y], preferred_element_type=F32).astype(BF16)
        else:
            if g == n:
                for copy in spread:
                    copy.wait_recv()
            held = slice(k0 * sl - rd0, k1 * sl - rd0)
            for yy in range(ny):
                snd4[yy, held, :] = jnp.dot(
                    sel[rows, :], nall[yy], preferred_element_type=F32
                ).astype(BF16)
        for k in range(k0, k1):
            at = pl.ds(k * sl, sl)
            if g < n:
                there[k] = move(k, snd.at[at], xg.at[c, y, at], (expert_at(k), t))
            else:
                held = pl.ds(k * sl - rd0, sl)
                there[k] = move(k, snd4.at[:, held], xg.at[c, :, at], (expert_at(k), t))

    def arrived(k, copies):
        if offsets[k] == (0, 0):
            copies[k].wait()
        else:
            copies[k].wait_recv()

    state_of = [dict() for _ in groups]

    def span(g):
        k0, k1 = groups[g]
        return k0 * sl, (k1 - k0) * sl

    def gather_first(g):
        s = state_of[g]
        r0, rn = span(g)
        for k in range(*groups[g]):
            arrived(k, there)
        if g >= n:
            block = xg.at[c, :, pl.ds(r0, rn)]
            s["near"] = [remote(block, block, sibling)]
            return
        block = xg.at[c, y, pl.ds(r0, rn)]
        s["b"] = remote(block, block, ahead)
        s["f"] = remote(block, block, behind)
        s["near"] = [remote(block, block, sibling)]

    def gather_second(g):
        s = state_of[g]
        r0, rn = span(g)
        s["b"].wait_recv()
        block = xg.at[c, yb, pl.ds(r0, rn)]
        s["o"] = remote(block, block, ahead)
        s["near"].append(remote(block, block, sibling))
        s["f"].wait_recv()
        block = xg.at[c, yf, pl.ds(r0, rn)]
        s["near"].append(remote(block, block, sibling))

    def gather_third(g):
        s = state_of[g]
        r0, rn = span(g)
        s["o"].wait_recv()
        block = xg.at[c, yo, pl.ds(r0, rn)]
        s["near"].append(remote(block, block, sibling))

    weights_here = []

    def compute(g):
        s = state_of[g]
        r0, rn = span(g)
        for copy in s["near"]:
            copy.wait_recv()
        if not weights_here:
            weights_here.append(True)
            for copy in w_loads:
                copy.wait()
        at = pl.ds(r0, rn)
        acc[:rn, :] = jnp.zeros((rn, 2 * f), F32)

        @pl.loop(0, nt)
        def _(j):
            w = wgu[pl.ds(pl.multiple_of(j * dc, dc), dc), :]
            acc[:rn, :] += jnp.dot(
                xg[lax.rem(j, 2), j // 2, at, :], w, preferred_element_type=F32
            )

        a = acc[:rn, :f]
        hid[:rn, :] = (a / (1.0 + jnp.exp(-a)) * acc[:rn, f:]).astype(BF16)

        @pl.loop(0, ny)
        def _(yy):
            sib[yy, at, :] = jnp.dot(
                hid[:rn, :], wdv[yy * 2 + 1 - c], preferred_element_type=F32
            ).astype(BF16)

        s["pair"] = remote(sib.at[:, at], rb.at[:, at], sibling)

        @pl.loop(0, ny)
        def _(yy):
            own[yy, at, :] = jnp.dot(
                hid[:rn, :], wdv[yy * 2 + c], preferred_element_type=F32
            ).astype(BF16)

    back_copies = [None] * experts

    def reduce_first(g):
        s = state_of[g]
        r0, rn = span(g)
        at = pl.ds(r0, rn)
        s["pair"].wait_recv()

        def pair(i):
            own[i, at, :] = own[i, at, :] + rb[i, at, :]

        if g >= n:
            for i in range(ny):
                pair(i)
            for k in range(*groups[g]):
                here = pl.ds(k * sl, sl)
                held = pl.ds(k * sl - rd0, sl)
                back_copies[k] = move(
                    k, own.at[:, here], back4.at[:, held], (expert_at(k, -1), t)
                )
            return
        pair(yo)
        s["t"] = remote(own.at[yo, at], tr.at[at], ahead)
        pair(yb)
        s["f1"] = remote(own.at[yb, at], fin.at[1, at], behind)
        pair(yf)
        pair(y)

    def reduce_second(g):
        s = state_of[g]
        r0, rn = span(g)
        at = pl.ds(r0, rn)
        s["t"].wait_recv()
        own[yf, at, :] = own[yf, at, :] + tr[at, :]
        s["f0"] = remote(own.at[yf, at], fin.at[0, at], ahead)

    def reduce_third(g):
        s = state_of[g]
        r0, rn = span(g)
        at = pl.ds(r0, rn)
        s["f1"].wait_recv()
        s["f0"].wait_recv()
        own[y, at, :] = (
            own[y, at, :].astype(F32) + fin[0, at, :].astype(F32) + fin[1, at, :].astype(F32)
        ).astype(BF16)
        for k in range(*groups[g]):
            here = pl.ds(k * sl, sl)
            back_copies[k] = move(k, own.at[y, here], back.at[here], (expert_at(k, -1), t))

    def combine(rows, values):
        return lax.dot_general(
            selw[rows, :], values, (((0,), (0,)), ((), ())), preferred_element_type=F32
        )

    summed = []

    def combine_direct(g):
        for k in range(kd, experts):
            arrived(k, back_copies)
        rows = slice(rd0, experts * sl)
        for i, (yy, peer) in enumerate(((yo, opposite), (yb, behind), (yf, ahead))):
            msd[i] = combine(rows, back4[yy]).astype(BF16)
            summed.append(remote(msd.at[i], mrd.at[i], peer))
        mine4[...] = combine(rows, back4[y])

    mixed_groups = []

    def combine_normal(g):
        for k in range(*groups[g]):
            arrived(k, back_copies)
        r0, rn = span(g)
        rows = slice(r0, r0 + rn)
        if mixed_groups:
            mix[...] += combine(rows, back[rows, :])
        else:
            mix[...] = combine(rows, back[rows, :])
        mixed_groups.append(g)

    def to_out(copies, buf, out):
        for copy in copies[0]:
            copy.wait_recv()
        copies[1].wait()
        for j in range(nt):
            out[:, j * dc : (j + 1) * dc] = buf[j]

    def residual_out(g):
        to_out(res_rows, rbuf, outs.at[0])

    steps = dict(
        P=dispatch, D=gather_first, F=gather_second, H=gather_third, C=compute,
        Q=reduce_first, T=reduce_second, U=reduce_third, A=spread_rows, V=combine_direct,
        W=combine_normal,
    )
    for name, g in schedule_of(n, len(direct)):
        steps[name](g)
        if name == "V":
            residual_out(g)

    mixed = mine4[...] + mix[...]
    for i, copy in enumerate(summed):
        copy.wait_recv()
        mixed = mixed + mrd[i].astype(F32)
    msend[...] = mixed.astype(BF16)
    done = list(sent)
    last = to_rows(msend, mbuf)
    for copy in done:
        copy.wait_send()
    to_out(last, mbuf, outs.at[1])
    for copy in sent[len(done) :]:
        copy.wait_send()


def shards(attn_partials, resid, norm_gain, expert_ids, gate_num, w_gate, w_up, w_down):
    experts = lax.axis_size("expert")
    nt = lax.axis_size("tensor")
    nx, nz = grid_of(experts)
    _, two, tokens, d = attn_partials.shape
    top = expert_ids.shape[-1]
    tg = two * tokens
    per = tg // nt
    dc = d // nt
    ny = nt // 2
    f = w_gate.shape[-1]
    cap = min(BLOCK, 3 * BLOCK * top // (2 * experts))
    sl = tg // BLOCK * cap
    rows = experts * sl
    normal, direct = groups_of(nx, nz)
    most = max(len(g) for g in normal + direct) * sl
    nrows = sum(len(g) for g in normal) * sl
    n_groups = len(normal + direct)

    n_remote = 4 + 3 + 2 * (experts - 1) + 3 * (nt - 1) + 12 * n_groups + ny + 8
    n_local = ny + 3 + nt + 4
    vmem = pl.BlockSpec(memory_space=pltpu.VMEM)
    hbm = pl.BlockSpec(memory_space=pl.ANY)
    scratch = [
        pltpu.VMEM((d, 2 * f), BF16),
        pltpu.VMEM((nt, f, dc), BF16),
        pltpu.VMEM((ny, tg, dc), BF16),
        pltpu.VMEM((ny, tg, dc), BF16),
        pltpu.VMEM((3, tg, dc), BF16),
        pltpu.VMEM((tg, dc), BF16),
        pltpu.VMEM((tg, dc), F32),
        pltpu.VMEM((ny, tg, dc), BF16),
        pltpu.VMEM((tg, dc), BF16),
        pltpu.VMEM((nt, per, dc), BF16),
        pltpu.VMEM((8, tg), F32),
        pltpu.VMEM((nt, 8, tg), F32),
        pltpu.VMEM((experts, tg), F32),
        pltpu.VMEM((experts, tg), F32),
        pltpu.VMEM((rows, tg), BF16),
        pltpu.VMEM((rows, tg), BF16),
        pltpu.VMEM((nrows, dc), BF16),
        pltpu.VMEM((ny, rows - nrows, dc), BF16),
        pltpu.VMEM((2, ny, rows, dc), BF16),
        pltpu.VMEM((most, 2 * f), F32),
        pltpu.VMEM((most, f), BF16),
        pltpu.VMEM((ny, rows, dc), BF16),
        pltpu.VMEM((ny, rows, dc), BF16),
        pltpu.VMEM((ny, rows, dc), BF16),
        pltpu.VMEM((nrows, dc), BF16),
        pltpu.VMEM((2, nrows, dc), BF16),
        pltpu.VMEM((nrows, dc), BF16),
        pltpu.VMEM((ny, rows - nrows, dc), BF16),
        pltpu.VMEM((3, tg, dc), BF16),
        pltpu.VMEM((3, tg, dc), BF16),
        pltpu.VMEM((tg, dc), F32),
        pltpu.VMEM((tg, dc), F32),
        pltpu.VMEM((tg, dc), BF16),
        pltpu.VMEM((nt, per, dc), BF16),
        pltpu.SemaphoreType.DMA((n_local,)),
        pltpu.SemaphoreType.DMA((n_remote,)),
        pltpu.SemaphoreType.DMA((n_remote,)),
    ]
    both = pl.pallas_call(
        functools.partial(kernel, (experts, nt, nx, nz, cap, d)),
        out_shape=jax.ShapeDtypeStruct((2, per, d), BF16),
        in_specs=[hbm, hbm, vmem, vmem, vmem, hbm, hbm, hbm],
        out_specs=vmem,
        scratch_shapes=scratch,
        compiler_params=pltpu.CompilerParams(
            collective_id=0, has_side_effects=True, vmem_limit_bytes=60 * 1024 * 1024
        ),
        cost_estimate=pl.CostEstimate(
            flops=6 * rows * d * f, bytes_accessed=6 * d * f, transcendentals=rows * f
        ),
    )(
        attn_partials.reshape(tg, d),
        resid.reshape(tg, d),
        norm_gain.reshape(1, d),
        expert_ids.transpose(0, 2, 1),
        gate_num.transpose(0, 2, 1),
        w_gate.reshape(d, f),
        w_up.reshape(d, f),
        w_down.reshape(f, d),
    )
    res, mix = both[0], both[1]
    return (res.reshape(two, per // two, d), mix.reshape(two, per // two, d))


def solution(mesh):
    placed = (
        P("tensor", None, "expert", None),
        P(None, "expert", None),
        P(),
        P(None, "expert", None),
        P(None, "expert", None),
        P("expert", None, "tensor"),
        P("expert", None, "tensor"),
        P("expert", "tensor", None),
    )
    return jax.shard_map(
        shards,
        mesh=mesh,
        in_specs=placed,
        out_specs=(P(None, ("expert", "tensor"), None), P(None, ("expert", "tensor"), None)),
        check_vma=False,
    )
```

time: 187 us -> 139 us (0.74)
  Pallas kernels: 179 us -> 136 us
  local copies, waits for them, and re-layouts: 7.57 us -> 1.68 us
    pallas_call x1, Pallas kernels: 179 us -> 136 us  [shards(): pl.pallas_call(functools.partial(kernel, (experts, nt, nx, nz, cap, d)),...]
    reshape x7 -> x0, local copies, waits for them, and re-layouts: 4.43 us -> none  [the longest x4 1.65 us: by_device(): a = a.reshape(two, nt, tokens // nt, top)]
    unnamed x2 -> x0, local copies, waits for them, and re-layouts: 3.14 us -> none
where the time goes in v2:
time: 139 us
  Pallas kernels  136 us (98%)
  local copies, waits for them, and re-layouts  1.68 us (1%)
    pallas_call x1, Pallas kernels, shards(): pl.pallas_call(functools.partial(kernel, (experts, nt, nx, nz, cap, d)),...  136 us

profile of v2, /device:TPU:1, one launch (start us, length us, event | category | flops | bytes accessed | tf_op | source)
XLA Modules:
  0.0 138.7 jit_solution(1924886473639282758)
XLA Ops:
  0.6 136.4 %shard_map.95 = bf16[2,16,4096]{2,1,0:T(8,128)(2,1)} custom-call(bf16[128,4096]{1,0:T(8,128)(2,1)} %bitcast.15, bf16[128,4096]{1,0:T(8,128)(2,1)} %bitcast.16, f32[1,4096]{1,0:T(1,128)} %bitcast.17, s32[2,8,64]{2,1,0:T(8,128)} %bitcast.18, s32[2,8,64]{2,1,0:T(8,128)} %bitcast.19, bf16[4096,384]{1,0:T(8,128)(2,1)} %bitcast.12, bf16[4096,384]{1,0:T(8,128)(2,1)} %bitcast.13, ...), custom_call_target="tpu_custom_call" | custom-call | flops 14495514624 | bytes 9437184 | tf_op jit(solution)/shard_map/pallas_call | solution.py:533
  137.0 1.7 %slice_bitcast_fusion = (bf16[2,8,4096]{2,1,0:T(8,128)(2,1)}, bf16[2,8,4096]{2,1,0:T(8,128)(2,1)}) fusion(bf16[2,16,4096]{2,1,0:T(8,128)(2,1)} %shard_map.95), kind=kLoop, calls=%fused_computation | loop fusion | bytes 524288 | tf_op jit(solution)/shard_map/reshape;squeeze | solution.py:556

commit v3 on v2

--- a/solution.py
+++ b/solution.py
@@ -31,9 +31,11 @@
     def offsets(name):
         far = int(name[1])
         if far in (0, nz - far):
-            return [(dx, far) for dx in range(nx)]
-        flip = name[0] == "B"
-        return [(dx, far if (dx < nx // 2) != flip else nz - far) for dx in range(nx)]
+            both = [(dx, far) for dx in range(nx)]
+            return both if name[0] == "A" else both[name[0] == "c" :: 2]
+        flip = name[0] in "Bbd"
+        both = [(dx, far if (dx < nx // 2) != flip else nz - far) for dx in range(nx)]
+        return both if name[0] in "AB" else both[name[0] in "cd" :: 2]
 
     if nx == 4 and nz == 8:
         return [offsets(a + b) for a, b in zip(NORMAL[::2], NORMAL[1::2])], [
@@ -57,7 +59,7 @@
     outs,
     wgu, wdv, ap, arb, afin, rsd, hs, nall, rsend, rbuf, ssend, sbuf,
     rank, gate, sel, selw, snd, snd4, xg, acc, hid, own, sib, rb, tr, fin, back, back4, msd, mrd, mine4, mix, msend, mbuf,
-    lsem, ssem, rsem,
+    lsem, ssem, rsem, ready,
 ):
     experts, nt, nx, nz, cap, d = cfg
     ny = nt // 2
@@ -118,7 +120,7 @@
     barrier = pltpu.get_barrier_semaphore()
     peers = 0
     for k, (dx, dz) in enumerate(offsets):
-        if (dx, dz) != (0, 0):
+        if (dx == 0) != (dz == 0):
             pl.semaphore_signal(barrier, inc=1, device_id=(expert_at(k), t), device_id_type=MESH)
             peers += 1
     for i in range(1, nt):
@@ -139,6 +141,10 @@
         copy.start()
 
     pl.semaphore_wait(barrier, peers)
+    for dx in range(1, nx):
+        pl.semaphore_signal(
+            ready, inc=1, device_id=(lax.rem(x + dx, nx) * nz + z, t), device_id_type=MESH
+        )
 
     a1 = [remote(cols(attn, 2 * yy + 1 - c), arb.at[yy], sibling) for yy in (yo, yf, yb, y)]
 
@@ -237,6 +243,8 @@
         at = slice(j * tg, (j + 1) * tg)
         nall[y, :, at] = (hs[:, at] * scale * mygain[:, at]).astype(BF16)
 
+    if nx > 1:
+        pl.semaphore_wait(ready, nx - 1)
     there = [None] * experts
 
     spread = []
@@ -332,12 +340,11 @@
         at = pl.ds(r0, rn)
         acc[:rn, :] = jnp.zeros((rn, 2 * f), F32)
 
-        @pl.loop(0, nt)
+        @pl.loop(0, ny)
         def _(j):
-            w = wgu[pl.ds(pl.multiple_of(j * dc, dc), dc), :]
-            acc[:rn, :] += jnp.dot(
-                xg[lax.rem(j, 2), j // 2, at, :], w, preferred_element_type=F32
-            )
+            w = wgu[pl.ds(pl.multiple_of(j * 2 * dc, 2 * dc), 2 * dc), :]
+            wide = jnp.concatenate([xg[0, j, at, :], xg[1, j, at, :]], axis=1)
+            acc[:rn, :] += jnp.dot(wide, w, preferred_element_type=F32)
 
         a = acc[:rn, :f]
         hid[:rn, :] = (a / (1.0 + jnp.exp(-a)) * acc[:rn, f:]).astype(BF16)
@@ -529,6 +536,7 @@
         pltpu.SemaphoreType.DMA((n_local,)),
         pltpu.SemaphoreType.DMA((n_remote,)),
         pltpu.SemaphoreType.DMA((n_remote,)),
+        pltpu.SemaphoreType.REGULAR,
     ]
     both = pl.pallas_call(
         functools.partial(kernel, (experts, nt, nx, nz, cap, d)),

time: 139 us -> 135 us (0.971)
  Pallas kernels: 136 us -> 133 us
    pallas_call x1, Pallas kernels: 136 us -> 133 us  [shards(): pl.pallas_call(functools.partial(kernel, (experts, nt, nx, nz, cap, d)),...]
where the time goes in v3:
time: 135 us
  Pallas kernels  133 us (99%)
  local copies, waits for them, and re-layouts  1.68 us (1%)
    pallas_call x1, Pallas kernels, shards(): pl.pallas_call(functools.partial(kernel, (experts, nt, nx, nz, cap, d)),...  133 us

profile of v3, /device:TPU:1, one launch (start us, length us, event | category | flops | bytes accessed | tf_op | source)
XLA Modules:
  0.0 134.9 jit_solution(17783965314740534775)
XLA Ops:
  0.6 132.6 %shard_map.95 = bf16[2,16,4096]{2,1,0:T(8,128)(2,1)} custom-call(bf16[128,4096]{1,0:T(8,128)(2,1)} %bitcast.15, bf16[128,4096]{1,0:T(8,128)(2,1)} %bitcast.16, f32[1,4096]{1,0:T(1,128)} %bitcast.17, s32[2,8,64]{2,1,0:T(8,128)} %bitcast.18, s32[2,8,64]{2,1,0:T(8,128)} %bitcast.19, bf16[4096,384]{1,0:T(8,128)(2,1)} %bitcast.12, bf16[4096,384]{1,0:T(8,128)(2,1)} %bitcast.13, ...), custom_call_target="tpu_custom_call" | custom-call | flops 14495514624 | bytes 9437184 | tf_op jit(solution)/shard_map/pallas_call | solution.py:541
  133.3 1.7 %slice_bitcast_fusion = (bf16[2,8,4096]{2,1,0:T(8,128)(2,1)}, bf16[2,8,4096]{2,1,0:T(8,128)(2,1)}) fusion(bf16[2,16,4096]{2,1,0:T(8,128)(2,1)} %shard_map.95), kind=kLoop, calls=%fused_computation | loop fusion | bytes 524288 | tf_op jit(solution)/shard_map/reshape;squeeze | solution.py:564
